TPU v7x, 32 devices: a whole 2x2x4 slice. The times are simulated.
32 devices in a mesh: band: 4 (over y, x), kpt: 8 (over z, core).
Axes of the slice: x: 2, y: 2, z: 4, core: 2. Of those that a mesh axis runs over, the one named last changes fastest.
Arguments:
- orbitals: bfloat16 [4, 8, 2, 32, 1024], P('band', 'kpt'), may hold values from -6 to 6
- kcoord: int32 [8, 3], replicated, may hold values from 0 to 7
Outputs:
- exchange: float32 [4, 8, 2, 32, 1024], P('band', 'kpt')
All inputs are finite; a program needn't handle non-finite values.
Results may differ from a plain program's by a relative error of at most 0.0003.
Values may be sent and summed in bfloat16 or wider, within the bound.
A program may use at most 64 MiB of HBM per device.

v0:
```python
import functools
import math

import jax
import jax.numpy as jnp
import numpy as np
from jax import lax
from jax.experimental import pallas as pl
from jax.experimental.pallas import tpu as pltpu
from jax.sharding import PartitionSpec as P

MESH = pl.DeviceIdType.MESH


def real_basis(grid, parity, freqs, points):
    angle = 2.0 * math.pi / grid * (np.outer(freqs, points) % grid)
    if parity == 0:
        return np.cos(angle)
    rows = np.sin(angle)
    for at, freq in enumerate(freqs):
        if freq == 0:
            rows[at] = np.cos(math.pi * np.asarray(points))
    return rows


def split(table):
    table = np.asarray(table, np.float32)
    high = table.astype(jnp.bfloat16)
    low = (table - high.astype(np.float32)).astype(jnp.bfloat16)
    return [high, low]


def groups(grid):
    half = grid // 2
    odd = list(range(1, half, 2))
    return [list(range(0, half, 4)), list(range(2, half, 4)), odd[: len(odd) // 2], odd[len(odd) // 2 :]]


def plane_table(grid, freqs, points):
    zline = list(range(grid))
    half = list(range(grid // 2))
    parts = []
    for yp in (0, 1):
        for zp in (0, 1):
            parts.append(np.kron(real_basis(grid, yp, freqs, points), real_basis(grid, zp, half, zline)).T)
    return np.concatenate(parts, axis=1)


def tables(grid):
    eighth = list(range(grid // 4))
    quarter = groups(grid)
    a = plane_table(grid, quarter[0], eighth)
    b = plane_table(grid, quarter[1], eighth)
    odd_points = list(range(grid // 2))
    c = np.concatenate([plane_table(grid, quarter[2], odd_points), plane_table(grid, quarter[3], odd_points)], axis=1)
    half = list(range(grid // 2))
    line = list(range(grid))
    x = np.concatenate([real_basis(grid, 0, half, line), real_basis(grid, 1, half, line)], axis=0)
    x = np.kron(np.eye(8), x)
    small = np.stack([t for m in (a, a.T, b, b.T, x, x.T) for t in split(m)])
    large = np.stack([t for m in (c, c.T) for t in split(m)])
    return small, large


def lane_table(grid):
    half = grid // 2
    rows = []
    for freqs in groups(grid):
        fy, fz = [], []
        for yp in (0, 1):
            for zp in (0, 1):
                for j in freqs:
                    for i in range(half):
                        fy.append(j if yp == 0 else (-j if j else -half))
                        fz.append(i if zp == 0 else (-i if i else -half))
        fy, fz = np.array(fy), np.array(fz)
        paired = [(f != 0) & (f != -half) for f in (fy, fz)]
        rows.append(np.stack([fy, fz, paired[0], paired[1]] + [np.zeros_like(fy)] * 4))
    return np.stack(rows).astype(np.float32)


def halves(a):
    high = a.astype(jnp.bfloat16)
    low = (a - high.astype(jnp.float32)).astype(jnp.bfloat16)
    return high, low


def dot(a, b):
    return jnp.dot(a, b, preferred_element_type=jnp.float32)


def right(a, high_table, low_table):
    high, low = halves(a)
    rows = a.shape[0]
    both = dot(jnp.concatenate([high, low], axis=0), high_table)
    return both[:rows] + (both[rows:] + dot(high, low_table))


def left(high_table, low_table, a):
    high, low = halves(a)
    return dot(high_table, high) + (dot(low_table, high) + dot(high_table, low))


def x_freq(grid, shape):
    half = grid // 2
    row = lax.broadcasted_iota(jnp.int32, shape, len(shape) - 2)
    freq = jnp.where(row < half, row, jnp.where(row == half, -half, half - row))
    return freq.astype(jnp.float32), jnp.where(row % half == 0, 0.0, 1.0).astype(jnp.float32)


def swap_x(a):
    half = a.shape[1] // 2
    return jnp.concatenate([a[:, half:], a[:, :half]], axis=1)


def swap_y(a):
    half = a.shape[2] // 2
    return jnp.concatenate([a[:, :, half:], a[:, :, :half]], axis=2)


def swap_z(a):
    half = a.shape[2] // 2
    parts = [pltpu.roll(a[:, :, at * half : (at + 1) * half], half // 2, 2) for at in (0, 1)]
    return jnp.concatenate(parts, axis=2)


def convolve(parts, kern, small, large, pairing):
    rows, lanes = parts[0].shape
    grid = rows // 2
    sum_02, sum_13 = parts[0] + parts[2], parts[1] + parts[3]
    odd = jnp.concatenate([parts[0] - parts[2], parts[1] - parts[3]], axis=1)
    freq_a = right(sum_02 + sum_13, small[0], small[1])
    freq_b = right(sum_02 - sum_13, small[4], small[5])
    freq_c = right(odd, large[0], large[1])
    field = jnp.concatenate([freq_a, freq_b, freq_c[:, :lanes], freq_c[:, lanes:]], axis=0)
    field = left(small[8], small[9], field)
    if pairing is None:
        field = (field.reshape(4, 2, grid, lanes) * kern[:, None]).reshape(4 * rows, lanes)
    else:
        field = field.reshape(4, 2, grid, lanes)
        re, im = field[:, 0], field[:, 1]
        for swap, paired in zip((swap_x, swap_y, swap_z), pairing):
            re, im = re + paired * swap(im), im - paired * swap(re)
        re, im = re * kern, im * kern
        for swap, paired in zip((swap_x, swap_y, swap_z), pairing):
            re, im = re - paired * swap(im), im + paired * swap(re)
        field = jnp.stack([re, im], axis=1).reshape(4 * rows, lanes)
    field = left(small[10], small[11], field)
    back_a = right(field[:rows], small[2], small[3])
    back_b = right(field[rows : 2 * rows], small[6], small[7])
    back_c = right(jnp.concatenate([field[2 * rows : 3 * rows], field[3 * rows :]], axis=1), large[2], large[3])
    even, alternate = back_a + back_b, back_a - back_b
    return [even + back_c[:, :lanes], alternate + back_c[:, lanes:], even - back_c[:, :lanes], alternate - back_c[:, lanes:]]


def band_partners(bands):
    if bands == 4:
        flip = lambda b: b + 1 - 2 * (b % 2)
        across = lambda b: (b + 2) % 4
        corner = lambda b: 3 - b
        return [(flip, flip, 1.0), (across, across, 2.0), (corner, corner, 1.0)]
    counts = {}
    for shift in (1, -1, 2, -2):
        counts[shift % bands] = counts.get(shift % bands, 0) + 1
    found = []
    for shift, times in counts.items():
        found.append((lambda b, s=shift: (b + s) % bands, lambda b, s=shift: (b + bands - s) % bands, float(times)))
    return found


def kernel(bands, kpts, kcoord_ref, own_hbm, small_hbm, large_hbm, lane_ref, out_ref, own, got, small, large, local_sems, send_sems, recv_sems):
    band = lax.axis_index("band")
    kpt = lax.axis_index("kpt")
    partners = band_partners(bands)
    later, earlier = (kpt + 1) % kpts, (kpt + kpts - 1) % kpts
    sources = [(band, later)] + [(src(band), kpt) for src, _, _ in partners]
    targets = [(band, earlier)] + [(dst(band), kpt) for _, dst, _ in partners]
    greeted = [(band, later)] + ([(band, earlier)] if kpts > 2 else [])
    if bands == 4:
        greeted += sources[1:]
    else:
        greeted += [((band + s) % bands, kpt) for s in sorted({s % bands for s in (1, -1, 2, -2)})]

    barrier = pltpu.get_barrier_semaphore()
    for device in greeted:
        pl.semaphore_signal(barrier, inc=1, device_id=device, device_id_type=MESH)
    fetches = [
        pltpu.make_async_copy(own_hbm, own, local_sems.at[0]),
        pltpu.make_async_copy(small_hbm, small, local_sems.at[1]),
        pltpu.make_async_copy(large_hbm, large, local_sems.at[2]),
    ]
    for fetch in fetches:
        fetch.start()
    pl.semaphore_wait(barrier, len(greeted))
    copies = []
    for at, device in enumerate(targets):
        copies.append(
            pltpu.make_async_remote_copy(
                src_ref=own_hbm,
                dst_ref=got.at[at],
                send_sem=send_sems.at[at],
                recv_sem=recv_sems.at[at],
                device_id=device,
                device_id_type=MESH,
            )
        )
    for at in list(range(1, len(targets) - 1)) + [0, len(targets) - 1]:
        copies[at].start()

    grid = own_hbm.shape[1]
    lanes = own_hbm.shape[2] // 4
    scale = -1.0 / float(grid**3)
    fx, x_paired = x_freq(grid, (1, grid, lanes))
    fy, fz = lane_ref[:, 0:1, :], lane_ref[:, 1:2, :]
    y_paired, z_paired = lane_ref[:, 2:3, :], lane_ref[:, 3:4, :]
    qx, qy, qz = [(kcoord_ref[later, i] - kcoord_ref[kpt, i]).astype(jnp.float32) for i in range(3)]
    weight = (1.0 + x_paired) * ((1.0 + y_paired) * (1.0 + z_paired)) * scale
    kern_zero = weight / (1.0 + (fx * fx + fy * fy + fz * fz) / 256.0)
    gx, gy, gz = fx + qx, fy + qy, fz + qz
    kern_next = scale / (1.0 + (gx * gx + gy * gy + gz * gz) / 256.0)

    for fetch in fetches:
        fetch.wait()
    times = [1.0] + [t for _, _, t in partners]
    for at in range(len(targets)):
        copies[at].wait_recv()
        parts = []
        for part in range(4):
            cut = slice(part * lanes, (part + 1) * lanes)
            own_re, own_im = own[0, :, cut].astype(jnp.float32), own[1, :, cut].astype(jnp.float32)
            re, im = got[at, 0, :, cut].astype(jnp.float32), got[at, 1, :, cut].astype(jnp.float32)
            parts.append(jnp.concatenate([re * own_re + im * own_im, re * own_im - im * own_re], axis=0))
        if at == 0:
            phi = convolve(parts, kern_next, small, large, (x_paired, y_paired, z_paired))
        else:
            phi = convolve(parts, kern_zero * times[at], small, large, None)
        for part in range(4):
            cut = slice(part * lanes, (part + 1) * lanes)
            re, im = got[at, 0, :, cut].astype(jnp.float32), got[at, 1, :, cut].astype(jnp.float32)
            phi_re, phi_im = phi[part][:grid], phi[part][grid:]
            term_re = re * phi_re - im * phi_im
            term_im = re * phi_im + im * phi_re
            if at > 0:
                term_re = term_re + out_ref[0, :, cut]
                term_im = term_im + out_ref[1, :, cut]
            out_ref[0, :, cut] = term_re
            out_ref[1, :, cut] = term_im
    for copy in copies:
        copy.wait_send()


def local(bands, kpts, orbitals, kcoord):
    own = orbitals[0, 0]
    grid, merged = own.shape[1:]
    small, large = tables(grid)
    lanes = lane_table(grid)
    count = 1 + len(band_partners(bands))
    anywhere = pl.BlockSpec(memory_space=pl.ANY)
    vmem = pl.BlockSpec(memory_space=pltpu.VMEM)
    out = pl.pallas_call(
        functools.partial(kernel, bands, kpts),
        out_shape=jax.ShapeDtypeStruct((2, grid, merged), jnp.float32),
        in_specs=[pl.BlockSpec(memory_space=pltpu.SMEM), anywhere, anywhere, anywhere, vmem],
        out_specs=vmem,
        scratch_shapes=[
            pltpu.VMEM(own.shape, jnp.bfloat16),
            pltpu.VMEM((count, *own.shape), jnp.bfloat16),
            pltpu.VMEM(small.shape, jnp.bfloat16),
            pltpu.VMEM(large.shape, jnp.bfloat16),
            pltpu.SemaphoreType.DMA((3,)),
            pltpu.SemaphoreType.DMA((count,)),
            pltpu.SemaphoreType.DMA((count,)),
        ],
        compiler_params=pltpu.CompilerParams(collective_id=0, has_side_effects=True, vmem_limit_bytes=40 * 1024 * 1024),
    )(kcoord, own, jnp.asarray(small), jnp.asarray(large), jnp.asarray(lanes))
    return out.reshape(1, 1, 2, grid, merged)


def solution(mesh):
    in_specs = (P("band", "kpt", None, None, None), P())
    out_specs = P("band", "kpt", None, None, None)
    body = functools.partial(local, mesh.shape["band"], mesh.shape["kpt"])
    return jax.shard_map(body, mesh=mesh, in_specs=in_specs, out_specs=out_specs, check_vma=False)
```

profile of v0, /device:TPU:0, one launch (start us, length us, event | category | flops | bytes accessed | tf_op | source)
XLA Modules:
  0.0 20.7 jit_solution(5848400034008713019)
XLA Ops:
  0.0 0.8 %copy.6.kcoord_ref = s32[8,3]{1,0:T(8,128)S(1)} copy(s32[8,3]{0,1:T(4,128)} %param.6) | data formatting | bytes 192 | tf_op args[1]
  0.8 0.0 copy-start
  0.8 1.6 %copy-done = bf16[4,512,512]{2,1,0:T(8,128)(2,1)S(1)} copy-done((bf16[4,512,512]{2,1,0:T(8,128)(2,1)S(1)}, bf16[4,512,512]{2,1,0:T(8,128)(2,1)}, u32[]{:S(2)}) %copy-start) | copy-done | bytes 2097176
  2.3 0.0 copy-start.1
  2.4 1.4 %copy-done.1 = bf16[12,256,256]{2,1,0:T(8,128)(2,1)S(1)} copy-done((bf16[12,256,256]{2,1,0:T(8,128)(2,1)S(1)}, bf16[12,256,256]{2,1,0:T(8,128)(2,1)}, u32[]{:S(2)}) %copy-start.1) | copy-done | bytes 1572888
  3.8 0.0 copy-start.2
  3.8 0.9 %copy-done.2 = bf16[1,1,2,32,1024]{4,3,2,1,0:T(8,128)(2,1)S(1)} copy-done((bf16[1,1,2,32,1024]{4,3,2,1,0:T(8,128)(2,1)S(1)}, bf16[1,1,2,32,1024]{4,3,2,1,0:T(8,128)(2,1)}, u32[]{:S(2)}) %copy-start.2) | copy-done | bytes 131096
  4.7 0.0 copy-start.3
  4.7 0.8 %copy-done.3 = f32[4,8,256]{2,1,0:T(8,128)S(1)} copy-done((f32[4,8,256]{2,1,0:T(8,128)S(1)}, f32[4,8,256]{2,1,0:T(8,128)}, u32[]{:S(2)}) %copy-start.3) | copy-done | bytes 32792
  5.4 14.6 %shard_map.55 = f32[2,32,1024]{2,1,0:T(8,128)S(1)} custom-call(s32[8,3]{1,0:T(8,128)S(1)} %copy.6.kcoord_ref, bf16[2,32,1024]{2,1,0:T(8,128)(2,1)S(1)} %bitcast.3, bf16[12,256,256]{2,1,0:T(8,128)(2,1)S(1)} %copy-done.1, bf16[4,512,512]{2,1,0:T(8,128)(2,1)S(1)} %copy-done, f32[4,8,256]{2,1,0:T(8,128)S(1)} %copy-done.3), custom_call_target="tpu_custom_call" | custom-call | tf_op jit(solution)/shard_map/pallas_call | solution.py:260
  20.0 0.7 %copy.8 = f32[1,1,2,32,1024]{4,3,2,1,0:T(8,128)} copy(f32[1,1,2,32,1024]{4,3,2,1,0:T(8,128)S(1)} %bitcast.2) | data formatting | bytes 524288
Async XLA Ops:
  0.8 1.6 %copy-start = (bf16[4,512,512]{2,1,0:T(8,128)(2,1)S(1)}, bf16[4,512,512]{2,1,0:T(8,128)(2,1)}, u32[]{:S(2)}) copy-start(bf16[4,512,512]{2,1,0:T(8,128)(2,1)} %constant.7.clone.large_hbm) | copy-start | bytes 6291460
  2.3 1.4 %copy-start.1 = (bf16[12,256,256]{2,1,0:T(8,128)(2,1)S(1)}, bf16[12,256,256]{2,1,0:T(8,128)(2,1)}, u32[]{:S(2)}) copy-start(bf16[12,256,256]{2,1,0:T(8,128)(2,1)} %constant.6.clone.small_hbm) | copy-start | bytes 4718596
  3.8 0.9 %copy-start.2 = (bf16[1,1,2,32,1024]{4,3,2,1,0:T(8,128)(2,1)S(1)}, bf16[1,1,2,32,1024]{4,3,2,1,0:T(8,128)(2,1)}, u32[]{:S(2)}) copy-start(bf16[1,1,2,32,1024]{4,3,2,1,0:T(8,128)(2,1)} %param.5) | copy-start | bytes 393220
  4.7 0.8 %copy-start.3 = (f32[4,8,256]{2,1,0:T(8,128)S(1)}, f32[4,8,256]{2,1,0:T(8,128)}, u32[]{:S(2)}) copy-start(f32[4,8,256]{2,1,0:T(8,128)} %constant.8.clone.lane_ref) | copy-start | bytes 98308
where the time goes:
time: 21 us; the launch traced here: 20.7 us
  Pallas kernels  14.6 us (70%)
  local copies, waits for them, and re-layouts  6.12 us (29%)
    pallas_call x1, Pallas kernels, local(): pl.pallas_call(functools.partial(kernel, bands, kpts), out_shape=jax.Shap...  14.6 us
    unnamed x10, local copies, waits for them, and re-layouts  6.12 us

commit v1 on v0

--- a/solution.py
+++ b/solution.py
@@ -10,6 +10,7 @@
 from jax.sharding import PartitionSpec as P
 
 MESH = pl.DeviceIdType.MESH
+VMEM_BYTES = 56 * 1024 * 1024
 
 
 def real_basis(grid, parity, freqs, points):
@@ -62,21 +63,19 @@
     return small, large
 
 
-def lane_table(grid):
-    half = grid // 2
-    rows = []
-    for freqs in groups(grid):
-        fy, fz = [], []
-        for yp in (0, 1):
-            for zp in (0, 1):
-                for j in freqs:
-                    for i in range(half):
-                        fy.append(j if yp == 0 else (-j if j else -half))
-                        fz.append(i if zp == 0 else (-i if i else -half))
-        fy, fz = np.array(fy), np.array(fz)
-        paired = [(f != 0) & (f != -half) for f in (fy, fz)]
-        rows.append(np.stack([fy, fz, paired[0], paired[1]] + [np.zeros_like(fy)] * 4))
-    return np.stack(rows).astype(np.float32)
+def lane_freqs(grid):
+    half, count = grid // 2, grid // 8
+    shape = (4, 1, 4 * count * half)
+    quarter = lax.broadcasted_iota(jnp.int32, shape, 0)
+    lane = lax.broadcasted_iota(jnp.int32, shape, 2)
+    at = (lane // half) % count
+    y = jnp.where(quarter < 2, 4 * at + 2 * quarter, 2 * at + 1 + 2 * count * (quarter - 2))
+    z = lane % half
+    found = []
+    for size, second in ((y, lane // (2 * count * half) > 0), (z, (lane // (count * half)) % 2 > 0)):
+        freq = jnp.where(second, jnp.where(size == 0, -half, -size), size)
+        found.append((freq.astype(jnp.float32), jnp.where(size == 0, 0.0, 1.0).astype(jnp.float32)))
+    return found
 
 
 def halves(a):
@@ -168,7 +167,7 @@
     return found
 
 
-def kernel(bands, kpts, kcoord_ref, own_hbm, small_hbm, large_hbm, lane_ref, out_ref, own, got, small, large, local_sems, send_sems, recv_sems):
+def kernel(bands, kpts, kcoord_hbm, own_hbm, small_hbm, large_hbm, out_ref, kcoord_ref, own, got, small, large, local_sems, send_sems, recv_sems):
     band = lax.axis_index("band")
     kpt = lax.axis_index("kpt")
     partners = band_partners(bands)
@@ -188,6 +187,7 @@
         pltpu.make_async_copy(own_hbm, own, local_sems.at[0]),
         pltpu.make_async_copy(small_hbm, small, local_sems.at[1]),
         pltpu.make_async_copy(large_hbm, large, local_sems.at[2]),
+        pltpu.make_async_copy(kcoord_hbm, kcoord_ref, local_sems.at[3]),
     ]
     for fetch in fetches:
         fetch.start()
@@ -211,16 +211,15 @@
     lanes = own_hbm.shape[2] // 4
     scale = -1.0 / float(grid**3)
     fx, x_paired = x_freq(grid, (1, grid, lanes))
-    fy, fz = lane_ref[:, 0:1, :], lane_ref[:, 1:2, :]
-    y_paired, z_paired = lane_ref[:, 2:3, :], lane_ref[:, 3:4, :]
-    qx, qy, qz = [(kcoord_ref[later, i] - kcoord_ref[kpt, i]).astype(jnp.float32) for i in range(3)]
+    (fy, y_paired), (fz, z_paired) = lane_freqs(grid)
+    for fetch in fetches:
+        fetch.wait()
+    qx, qy, qz = [(kcoord_ref[i, later] - kcoord_ref[i, kpt]).astype(jnp.float32) for i in range(3)]
     weight = (1.0 + x_paired) * ((1.0 + y_paired) * (1.0 + z_paired)) * scale
     kern_zero = weight / (1.0 + (fx * fx + fy * fy + fz * fz) / 256.0)
     gx, gy, gz = fx + qx, fy + qy, fz + qz
     kern_next = scale / (1.0 + (gx * gx + gy * gy + gz * gz) / 256.0)
 
-    for fetch in fetches:
-        fetch.wait()
     times = [1.0] + [t for _, _, t in partners]
     for at in range(len(targets)):
         copies[at].wait_recv()
@@ -253,26 +252,26 @@
     own = orbitals[0, 0]
     grid, merged = own.shape[1:]
     small, large = tables(grid)
-    lanes = lane_table(grid)
     count = 1 + len(band_partners(bands))
-    anywhere = pl.BlockSpec(memory_space=pl.ANY)
+    hbm = pl.BlockSpec(memory_space=pltpu.HBM)
     vmem = pl.BlockSpec(memory_space=pltpu.VMEM)
     out = pl.pallas_call(
         functools.partial(kernel, bands, kpts),
-        out_shape=jax.ShapeDtypeStruct((2, grid, merged), jnp.float32),
-        in_specs=[pl.BlockSpec(memory_space=pltpu.SMEM), anywhere, anywhere, anywhere, vmem],
+        out_shape=pltpu.VMEM((2, grid, merged), jnp.float32),
+        in_specs=[hbm, hbm, hbm, hbm],
         out_specs=vmem,
         scratch_shapes=[
+            pltpu.SMEM(kcoord.T.shape, jnp.int32),
             pltpu.VMEM(own.shape, jnp.bfloat16),
             pltpu.VMEM((count, *own.shape), jnp.bfloat16),
             pltpu.VMEM(small.shape, jnp.bfloat16),
             pltpu.VMEM(large.shape, jnp.bfloat16),
-            pltpu.SemaphoreType.DMA((3,)),
+            pltpu.SemaphoreType.DMA((4,)),
             pltpu.SemaphoreType.DMA((count,)),
             pltpu.SemaphoreType.DMA((count,)),
         ],
-        compiler_params=pltpu.CompilerParams(collective_id=0, has_side_effects=True, vmem_limit_bytes=40 * 1024 * 1024),
-    )(kcoord, own, jnp.asarray(small), jnp.asarray(large), jnp.asarray(lanes))
+        compiler_params=pltpu.CompilerParams(collective_id=0, has_side_effects=True, vmem_limit_bytes=VMEM_BYTES),
+    )(kcoord.T, own, jnp.asarray(small), jnp.asarray(large))
     return out.reshape(1, 1, 2, grid, merged)
 
 

time: 21 us -> 15 us (0.71)
  local copies, waits for them, and re-layouts: 6.12 us -> 0.71 us
  Pallas kernels: 14.6 us -> 14.2 us
    unnamed x10 -> x1, local copies, waits for them, and re-layouts: 6.12 us -> 0.71 us
    pallas_call x1, Pallas kernels: 14.6 us -> 14.2 us  [local(): pl.pallas_call(functools.partial(kernel, bands, kpts), out_shape=pltpu.VM...]
where the time goes in v1:
time: 15 us; the launch traced here: 14.9 us
  Pallas kernels  14.2 us (95%)
  local copies, waits for them, and re-layouts  0.71 us (5%)
    pallas_call x1, Pallas kernels, local(): pl.pallas_call(functools.partial(kernel, bands, kpts), out_shape=pltpu.VM...  14.2 us
    unnamed x1, local copies, waits for them, and re-layouts  0.71 us

profile of v1, /device:TPU:0, one launch (start us, length us, event | category | flops | bytes accessed | tf_op | source)
XLA Modules:
  0.0 14.9 jit_solution(4575455330415028874)
XLA Ops:
  0.0 14.2 %shard_map.46 = f32[2,32,1024]{2,1,0:T(8,128)S(1)} custom-call(s32[3,8]{1,0:T(4,128)} %bitcast.5, bf16[2,32,1024]{2,1,0:T(8,128)(2,1)} %bitcast.4, bf16[12,256,256]{2,1,0:T(8,128)(2,1)} %constant.4.clone.small_hbm, bf16[4,512,512]{2,1,0:T(8,128)(2,1)} %constant.5.clone.large_hbm), custom_call_target="tpu_custom_call" | custom-call | tf_op jit(solution)/shard_map/pallas_call | solution.py:258
  14.2 0.7 %copy.6 = f32[1,1,2,32,1024]{4,3,2,1,0:T(8,128)} copy(f32[1,1,2,32,1024]{4,3,2,1,0:T(8,128)S(1)} %bitcast.3) | data formatting | bytes 524288

commit v2 on v1

--- a/solution.py
+++ b/solution.py
@@ -57,8 +57,11 @@
     half = list(range(grid // 2))
     line = list(range(grid))
     x = np.concatenate([real_basis(grid, 0, half, line), real_basis(grid, 1, half, line)], axis=0)
-    x = np.kron(np.eye(8), x)
-    small = np.stack([t for m in (a, a.T, b, b.T, x, x.T) for t in split(m)])
+    x_sides = np.zeros(a.shape, jnp.bfloat16)
+    for at, side in enumerate((x, x.T)):
+        high, low = split(np.kron(np.eye(2), side))
+        x_sides[at * 2 * grid : (at + 1) * 2 * grid, : 6 * grid] = np.concatenate([high, low, high], axis=1)
+    small = np.stack([t for m in (a, a.T, b, b.T) for t in split(m)] + [x_sides])
     large = np.stack([t for m in (c, c.T) for t in split(m)])
     return small, large
 
@@ -95,9 +98,14 @@
     return both[:rows] + (both[rows:] + dot(high, low_table))
 
 
-def left(high_table, low_table, a):
+def left(side, a):
     high, low = halves(a)
-    return dot(high_table, high) + (dot(low_table, high) + dot(high_table, low))
+    rows = side.shape[0]
+    done = []
+    for at in range(0, a.shape[0], rows):
+        cut = slice(at, at + rows)
+        done.append(dot(side, jnp.concatenate([high[cut], high[cut], low[cut]], axis=0)))
+    return jnp.concatenate(done, axis=0)
 
 
 def x_freq(grid, shape):
@@ -123,62 +131,61 @@
     return jnp.concatenate(parts, axis=2)
 
 
-def convolve(parts, kern, small, large, pairing):
-    rows, lanes = parts[0].shape
+def pairing_butterflies(field, paired, sign):
+    re, im = field
+    for swap, mask in zip((swap_x, swap_y, swap_z), paired):
+        mask = sign * mask
+        re, im = re + mask * swap(im), im - mask * swap(re)
+    return re, im
+
+
+def convolve(parts, kerns, small, large, paired):
+    lanes = parts[0].shape[1]
+    rows = parts[0].shape[0] // len(kerns)
     grid = rows // 2
     sum_02, sum_13 = parts[0] + parts[2], parts[1] + parts[3]
     odd = jnp.concatenate([parts[0] - parts[2], parts[1] - parts[3]], axis=1)
     freq_a = right(sum_02 + sum_13, small[0], small[1])
     freq_b = right(sum_02 - sum_13, small[4], small[5])
     freq_c = right(odd, large[0], large[1])
-    field = jnp.concatenate([freq_a, freq_b, freq_c[:, :lanes], freq_c[:, lanes:]], axis=0)
-    field = left(small[8], small[9], field)
-    if pairing is None:
-        field = (field.reshape(4, 2, grid, lanes) * kern[:, None]).reshape(4 * rows, lanes)
-    else:
-        field = field.reshape(4, 2, grid, lanes)
-        re, im = field[:, 0], field[:, 1]
-        for swap, paired in zip((swap_x, swap_y, swap_z), pairing):
-            re, im = re + paired * swap(im), im - paired * swap(re)
-        re, im = re * kern, im * kern
-        for swap, paired in zip((swap_x, swap_y, swap_z), pairing):
-            re, im = re - paired * swap(im), im + paired * swap(re)
-        field = jnp.stack([re, im], axis=1).reshape(4 * rows, lanes)
-    field = left(small[10], small[11], field)
-    back_a = right(field[:rows], small[2], small[3])
-    back_b = right(field[rows : 2 * rows], small[6], small[7])
-    back_c = right(jnp.concatenate([field[2 * rows : 3 * rows], field[3 * rows :]], axis=1), large[2], large[3])
+    fields = []
+    for at, (kern, shifted) in enumerate(kerns):
+        cut = slice(at * rows, (at + 1) * rows)
+        field = jnp.concatenate([freq_a[cut], freq_b[cut], freq_c[cut, :lanes], freq_c[cut, lanes:]], axis=0)
+        field = left(small[8, :rows, : 3 * rows], field).reshape(4, 2, grid, lanes)
+        if shifted:
+            re, im = pairing_butterflies((field[:, 0], field[:, 1]), paired, 1.0)
+            re, im = pairing_butterflies((re * kern, im * kern), paired, -1.0)
+            field = jnp.stack([re, im], axis=1)
+        else:
+            field = field * kern[:, None]
+        fields.append(left(small[8, rows : 2 * rows, : 3 * rows], field.reshape(4 * rows, lanes)))
+    quarters = [jnp.concatenate([f[q * rows : (q + 1) * rows] for f in fields], axis=0) for q in range(4)]
+    back_a = right(quarters[0], small[2], small[3])
+    back_b = right(quarters[1], small[6], small[7])
+    back_c = right(jnp.concatenate(quarters[2:], axis=1), large[2], large[3])
     even, alternate = back_a + back_b, back_a - back_b
     return [even + back_c[:, :lanes], alternate + back_c[:, lanes:], even - back_c[:, :lanes], alternate - back_c[:, lanes:]]
 
 
-def band_partners(bands):
-    if bands == 4:
-        flip = lambda b: b + 1 - 2 * (b % 2)
-        across = lambda b: (b + 2) % 4
-        corner = lambda b: 3 - b
-        return [(flip, flip, 1.0), (across, across, 2.0), (corner, corner, 1.0)]
+def band_shifts(bands):
     counts = {}
     for shift in (1, -1, 2, -2):
         counts[shift % bands] = counts.get(shift % bands, 0) + 1
-    found = []
-    for shift, times in counts.items():
-        found.append((lambda b, s=shift: (b + s) % bands, lambda b, s=shift: (b + bands - s) % bands, float(times)))
-    return found
-
-
-def kernel(bands, kpts, kcoord_hbm, own_hbm, small_hbm, large_hbm, out_ref, kcoord_ref, own, got, small, large, local_sems, send_sems, recv_sems):
+    return counts
+
+
+def kernel(bands, kpts, times, kcoord_hbm, own_hbm, small_hbm, large_hbm, out_ref, kcoord_ref, own, got, small, large, local_sems, send_sems, recv_sems):
     band = lax.axis_index("band")
     kpt = lax.axis_index("kpt")
-    partners = band_partners(bands)
     later, earlier = (kpt + 1) % kpts, (kpt + kpts - 1) % kpts
-    sources = [(band, later)] + [(src(band), kpt) for src, _, _ in partners]
-    targets = [(band, earlier)] + [(dst(band), kpt) for _, dst, _ in partners]
     greeted = [(band, later)] + ([(band, earlier)] if kpts > 2 else [])
     if bands == 4:
-        greeted += sources[1:]
+        flip = (band + 1 - 2 * (band % 2), kpt)
+        across = ((band + 2) % 4, kpt)
+        greeted += [flip, across, (3 - band, kpt)]
     else:
-        greeted += [((band + s) % bands, kpt) for s in sorted({s % bands for s in (1, -1, 2, -2)})]
+        greeted += [((band + shift) % bands, kpt) for shift in band_shifts(bands)]
 
     barrier = pltpu.get_barrier_semaphore()
     for device in greeted:
@@ -192,20 +199,31 @@
     for fetch in fetches:
         fetch.start()
     pl.semaphore_wait(barrier, len(greeted))
-    copies = []
-    for at, device in enumerate(targets):
-        copies.append(
-            pltpu.make_async_remote_copy(
-                src_ref=own_hbm,
-                dst_ref=got.at[at],
-                send_sem=send_sems.at[at],
-                recv_sem=recv_sems.at[at],
-                device_id=device,
-                device_id_type=MESH,
-            )
+    sent = []
+
+    def send(src, dst, device):
+        at = len(sent)
+        copy = pltpu.make_async_remote_copy(
+            src_ref=src,
+            dst_ref=dst,
+            send_sem=send_sems.at[at],
+            recv_sem=recv_sems.at[at],
+            device_id=device,
+            device_id_type=MESH,
         )
-    for at in list(range(1, len(targets) - 1)) + [0, len(targets) - 1]:
-        copies[at].start()
+        copy.start()
+        sent.append(copy)
+        return copy
+
+    if bands == 4:
+        corner = (3 - band, kpt)
+        awaited = {at: [send(own_hbm, got.at[at], device)] for at, device in ((1, flip), (2, across), (0, (band, earlier)), (3, corner))}
+        groups_of = [[0], [1, 2], [3]]
+    else:
+        awaited = {0: [send(own_hbm, got.at[0], (band, earlier))]}
+        for at, shift in enumerate(band_shifts(bands)):
+            awaited[at + 1] = [send(own_hbm, got.at[at + 1], ((band + bands - shift) % bands, kpt))]
+        groups_of = [[0], list(range(1, len(times)))]
 
     grid = own_hbm.shape[1]
     lanes = own_hbm.shape[2] // 4
@@ -220,31 +238,36 @@
     gx, gy, gz = fx + qx, fy + qy, fz + qz
     kern_next = scale / (1.0 + (gx * gx + gy * gy + gz * gz) / 256.0)
 
-    times = [1.0] + [t for _, _, t in partners]
-    for at in range(len(targets)):
-        copies[at].wait_recv()
+    rows = 2 * grid
+    for group in groups_of:
+        for at in group:
+            for copy in awaited[at]:
+                copy.wait_recv()
         parts = []
         for part in range(4):
             cut = slice(part * lanes, (part + 1) * lanes)
             own_re, own_im = own[0, :, cut].astype(jnp.float32), own[1, :, cut].astype(jnp.float32)
-            re, im = got[at, 0, :, cut].astype(jnp.float32), got[at, 1, :, cut].astype(jnp.float32)
-            parts.append(jnp.concatenate([re * own_re + im * own_im, re * own_im - im * own_re], axis=0))
-        if at == 0:
-            phi = convolve(parts, kern_next, small, large, (x_paired, y_paired, z_paired))
-        else:
-            phi = convolve(parts, kern_zero * times[at], small, large, None)
+            rho = []
+            for at in group:
+                re, im = got[at, 0, :, cut].astype(jnp.float32), got[at, 1, :, cut].astype(jnp.float32)
+                rho += [re * own_re + im * own_im, re * own_im - im * own_re]
+            parts.append(jnp.concatenate(rho, axis=0))
+        kerns = [(kern_zero * times[at], False) if at > 0 else (kern_next, True) for at in group]
+        phi = convolve(parts, kerns, small, large, (x_paired, y_paired, z_paired))
         for part in range(4):
             cut = slice(part * lanes, (part + 1) * lanes)
-            re, im = got[at, 0, :, cut].astype(jnp.float32), got[at, 1, :, cut].astype(jnp.float32)
-            phi_re, phi_im = phi[part][:grid], phi[part][grid:]
-            term_re = re * phi_re - im * phi_im
-            term_im = re * phi_im + im * phi_re
-            if at > 0:
-                term_re = term_re + out_ref[0, :, cut]
-                term_im = term_im + out_ref[1, :, cut]
-            out_ref[0, :, cut] = term_re
-            out_ref[1, :, cut] = term_im
-    for copy in copies:
+            total_re, total_im = [], []
+            if group != groups_of[0]:
+                total_re, total_im = [out_ref[0, :, cut]], [out_ref[1, :, cut]]
+            for place, at in enumerate(group):
+                re, im = got[at, 0, :, cut].astype(jnp.float32), got[at, 1, :, cut].astype(jnp.float32)
+                phi_re = phi[part][place * rows : place * rows + grid]
+                phi_im = phi[part][place * rows + grid : (place + 1) * rows]
+                total_re.append(re * phi_re - im * phi_im)
+                total_im.append(re * phi_im + im * phi_re)
+            out_ref[0, :, cut] = sum(total_re[1:], total_re[0])
+            out_ref[1, :, cut] = sum(total_im[1:], total_im[0])
+    for copy in sent:
         copy.wait_send()
 
 
@@ -252,23 +275,25 @@
     own = orbitals[0, 0]
     grid, merged = own.shape[1:]
     small, large = tables(grid)
-    count = 1 + len(band_partners(bands))
+    counts = band_shifts(bands)
+    times = [1.0, 1.0, 2.0, 1.0] if bands == 4 else [1.0] + [float(c) for c in counts.values()]
+    sends = len(times)
     hbm = pl.BlockSpec(memory_space=pltpu.HBM)
     vmem = pl.BlockSpec(memory_space=pltpu.VMEM)
     out = pl.pallas_call(
-        functools.partial(kernel, bands, kpts),
+        functools.partial(kernel, bands, kpts, times),
         out_shape=pltpu.VMEM((2, grid, merged), jnp.float32),
         in_specs=[hbm, hbm, hbm, hbm],
         out_specs=vmem,
         scratch_shapes=[
             pltpu.SMEM(kcoord.T.shape, jnp.int32),
             pltpu.VMEM(own.shape, jnp.bfloat16),
-            pltpu.VMEM((count, *own.shape), jnp.bfloat16),
+            pltpu.VMEM((len(times), *own.shape), jnp.bfloat16),
             pltpu.VMEM(small.shape, jnp.bfloat16),
             pltpu.VMEM(large.shape, jnp.bfloat16),
             pltpu.SemaphoreType.DMA((4,)),
-            pltpu.SemaphoreType.DMA((count,)),
-            pltpu.SemaphoreType.DMA((count,)),
+            pltpu.SemaphoreType.DMA((sends,)),
+            pltpu.SemaphoreType.DMA((sends,)),
         ],
         compiler_params=pltpu.CompilerParams(collective_id=0, has_side_effects=True, vmem_limit_bytes=VMEM_BYTES),
     )(kcoord.T, own, jnp.asarray(small), jnp.asarray(large))

time: 15 us -> 14.3 us (0.953)
  Pallas kernels: 14.2 us -> 13.4 us
    pallas_call x1, Pallas kernels: 14.2 us -> 13.4 us  [local(): pl.pallas_call(functools.partial(kernel, bands, kpts, times), out_shape=p...]
where the time goes in v2:
time: 14.3 us; the launch traced here: 14.2 us
  Pallas kernels  13.4 us (94%)
  local copies, waits for them, and re-layouts  0.71 us (5%)
    pallas_call x1, Pallas kernels, local(): pl.pallas_call(functools.partial(kernel, bands, kpts, times), out_shape=p...  13.4 us
    unnamed x1, local copies, waits for them, and re-layouts  0.71 us

profile of v2, /device:TPU:0, one launch (start us, length us, event | category | flops | bytes accessed | tf_op | source)
XLA Modules:
  0.0 14.2 jit_solution(15339619970341219461)
XLA Ops:
  0.0 13.4 %shard_map.46 = f32[2,32,1024]{2,1,0:T(8,128)S(1)} custom-call(s32[3,8]{1,0:T(4,128)} %bitcast.5, bf16[2,32,1024]{2,1,0:T(8,128)(2,1)} %bitcast.4, bf16[9,256,256]{2,1,0:T(8,128)(2,1)} %constant.4.clone.small_hbm, bf16[4,512,512]{2,1,0:T(8,128)(2,1)} %constant.5.clone.large_hbm), custom_call_target="tpu_custom_call" | custom-call | tf_op jit(solution)/shard_map/pallas_call | solution.py:283
  13.5 0.7 %copy.6 = f32[1,1,2,32,1024]{4,3,2,1,0:T(8,128)} copy(f32[1,1,2,32,1024]{4,3,2,1,0:T(8,128)S(1)} %bitcast.3) | data formatting | bytes 524288

commit v3 on v2

--- a/solution.py
+++ b/solution.py
@@ -200,6 +200,7 @@
         fetch.start()
     pl.semaphore_wait(barrier, len(greeted))
     sent = []
+    fetches[0].wait()
 
     def send(src, dst, device):
         at = len(sent)
@@ -217,12 +218,21 @@
 
     if bands == 4:
         corner = (3 - band, kpt)
-        awaited = {at: [send(own_hbm, got.at[at], device)] for at, device in ((1, flip), (2, across), (0, (band, earlier)), (3, corner))}
+        half = own_hbm.shape[1] // 2
+        first, second = slice(0, half), slice(half, 2 * half)
+        by_flip = send(own.at[1, first], got.at[1, 1, first], flip)
+        by_across = send(own.at[1, second], got.at[2, 1, second], across)
+        awaited = {
+            1: [send(own.at[0], got.at[1, 0], flip), send(own.at[1, second], got.at[1, 1, second], flip)],
+            2: [send(own.at[0], got.at[2, 0], across), send(own.at[1, first], got.at[2, 1, first], across)],
+            0: [send(own, got.at[0], (band, earlier))],
+            3: [send(own.at[0], got.at[3, 0], corner)],
+        }
         groups_of = [[0], [1, 2], [3]]
     else:
-        awaited = {0: [send(own_hbm, got.at[0], (band, earlier))]}
+        awaited = {0: [send(own, got.at[0], (band, earlier))]}
         for at, shift in enumerate(band_shifts(bands)):
-            awaited[at + 1] = [send(own_hbm, got.at[at + 1], ((band + bands - shift) % bands, kpt))]
+            awaited[at + 1] = [send(own, got.at[at + 1], ((band + bands - shift) % bands, kpt))]
         groups_of = [[0], list(range(1, len(times)))]
 
     grid = own_hbm.shape[1]
@@ -230,7 +240,7 @@
     scale = -1.0 / float(grid**3)
     fx, x_paired = x_freq(grid, (1, grid, lanes))
     (fy, y_paired), (fz, z_paired) = lane_freqs(grid)
-    for fetch in fetches:
+    for fetch in fetches[1:]:
         fetch.wait()
     qx, qy, qz = [(kcoord_ref[i, later] - kcoord_ref[i, kpt]).astype(jnp.float32) for i in range(3)]
     weight = (1.0 + x_paired) * ((1.0 + y_paired) * (1.0 + z_paired)) * scale
@@ -238,6 +248,11 @@
     gx, gy, gz = fx + qx, fy + qy, fz + qz
     kern_next = scale / (1.0 + (gx * gx + gy * gy + gz * gz) / 256.0)
 
+    if bands == 4:
+        by_flip.wait_recv()
+        awaited[3].append(send(got.at[1, 1, first], got.at[3, 1, first], across))
+        by_across.wait_recv()
+        awaited[3].append(send(got.at[2, 1, second], got.at[3, 1, second], flip))
     rows = 2 * grid
     for group in groups_of:
         for at in group:
@@ -277,7 +292,7 @@
     small, large = tables(grid)
     counts = band_shifts(bands)
     times = [1.0, 1.0, 2.0, 1.0] if bands == 4 else [1.0] + [float(c) for c in counts.values()]
-    sends = len(times)
+    sends = 10 if bands == 4 else len(times)
     hbm = pl.BlockSpec(memory_space=pltpu.HBM)
     vmem = pl.BlockSpec(memory_space=pltpu.VMEM)
     out = pl.pallas_call(

time: 14.3 us -> 13.9 us (0.972)
  Pallas kernels: 13.4 us -> 13 us
    pallas_call x1, Pallas kernels: 13.4 us -> 13 us  [local(): pl.pallas_call(functools.partial(kernel, bands, kpts, times), out_shape=p...]
where the time goes in v3:
time: 13.9 us; the launch traced here: 13.7 us
  Pallas kernels  13 us (94%)
  local copies, waits for them, and re-layouts  0.71 us (5%)
    pallas_call x1, Pallas kernels, local(): pl.pallas_call(functools.partial(kernel, bands, kpts, times), out_shape=p...  13 us
    unnamed x1, local copies, waits for them, and re-layouts  0.71 us

profile of v3, /device:TPU:0, one launch (start us, length us, event | category | flops | bytes accessed | tf_op | source)
XLA Modules:
  0.0 13.7 jit_solution(15415264501589391779)
XLA Ops:
  0.0 13.0 %shard_map.46 = f32[2,32,1024]{2,1,0:T(8,128)S(1)} custom-call(s32[3,8]{1,0:T(4,128)} %bitcast.5, bf16[2,32,1024]{2,1,0:T(8,128)(2,1)} %bitcast.4, bf16[9,256,256]{2,1,0:T(8,128)(2,1)} %constant.4.clone.small_hbm, bf16[4,512,512]{2,1,0:T(8,128)(2,1)} %constant.5.clone.large_hbm), custom_call_target="tpu_custom_call" | custom-call | tf_op jit(solution)/shard_map/pallas_call | solution.py:298
  13.0 0.7 %copy.6 = f32[1,1,2,32,1024]{4,3,2,1,0:T(8,128)} copy(f32[1,1,2,32,1024]{4,3,2,1,0:T(8,128)S(1)} %bitcast.3) | data formatting | bytes 524288
